TPU v7x, 512 devices: a whole 4x4x16 slice. The times are simulated.
512 devices in a mesh: expert: 64 (over x, z), tensor: 8 (over y, core).
Axes of the slice: x: 4, y: 4, z: 16, core: 2. Of those that a mesh axis runs over, the one named last changes fastest.
Arguments:
- first_half: bfloat16 [8192, 2048], P('expert', 'tensor'), may hold values from -6 to 6
- second_half: bfloat16 [8192, 2048], P('expert', 'tensor'), may hold values from -1.5 to 1.5
- first_grad: bfloat16 [8192, 2048], P('expert', 'tensor'), may hold values from -1.5 to 1.5
- second_grad: bfloat16 [8192, 2048], P('expert', 'tensor'), may hold values from -6 to 6
- expert_ids: int32 [8192, 6], P('expert'), may hold values from 0 to 63, as said below
- gate_weights: bfloat16 [8192, 6], P('expert'), may hold values from 0.049804688 to 0.5
- expert_in: bfloat16 [64, 2, 1408, 2048], P('expert', None, 'tensor'), may hold values from -0.125 to 0.125
- expert_out: bfloat16 [64, 1408, 2048], P('expert', 'tensor'), may hold values from -0.15625 to 0.15625
Outputs:
- restored: bfloat16 [8192, 2048], P('expert', 'tensor')
- carried_grad: bfloat16 [8192, 2048], P('expert', 'tensor')
- gate_grad: float32 [8192, 6], P('expert')
- grad_in: bfloat16 [64, 2, 1408, 2048], P('expert', None, 'tensor')
- grad_out: bfloat16 [64, 1408, 2048], P('expert', 'tensor')
Inputs may be any that keep to these rules, and one draw needn't show every extreme that they name: `expert_ids`: each token names 6 different experts. In the rows of one index of expert (128 tokens) each expert is named by at least 10 and at most 14 tokens, and one expert is named by exactly 14 tokens of every index of expert.
All inputs are finite; a program needn't handle non-finite values.
Results may differ from a plain program's by a relative error of at most 0.02.
Values may be sent and summed in bfloat16 or wider, within the bound.
A program may use at most 128 MiB of HBM per device.

v0:
```python
import jax
import jax.numpy as jnp
from jax import lax
from jax.sharding import PartitionSpec as P


def expert_work(slot_rows, slot_cots, slot_gates, weights_in, weights_out):
    pre = jnp.einsum("erd,ekhd->ekrh", slot_rows, weights_in, preferred_element_type=jnp.float32)
    gate_pre = pre[:, 0]
    up_pre = pre[:, 1]
    sigma = jax.nn.sigmoid(gate_pre)
    active = gate_pre * sigma
    hidden = (active * up_pre).astype(jnp.bfloat16)
    part_out = jnp.einsum("erh,ehd->erd", hidden, weights_out, preferred_element_type=jnp.float32)
    gate_piece = jnp.sum(slot_cots.astype(jnp.float32) * part_out, axis=2)
    scaled = (slot_gates[:, :, None].astype(jnp.float32) * slot_cots.astype(jnp.float32)).astype(
        jnp.bfloat16
    )
    hidden_grad = jnp.einsum(
        "erd,ehd->erh", scaled, weights_out, preferred_element_type=jnp.float32
    )
    gate_pre_grad = (hidden_grad * up_pre * sigma * (1.0 + gate_pre * (1.0 - sigma))).astype(
        jnp.bfloat16
    )
    up_grad = (hidden_grad * active).astype(jnp.bfloat16)
    input_piece = jnp.einsum(
        "erh,ehd->erd", gate_pre_grad, weights_in[:, 0], preferred_element_type=jnp.float32
    ) + jnp.einsum("erh,ehd->erd", up_grad, weights_in[:, 1], preferred_element_type=jnp.float32)
    grad_gate = jnp.einsum(
        "erh,erd->ehd", gate_pre_grad, slot_rows, preferred_element_type=jnp.float32
    ).astype(jnp.bfloat16)
    grad_up = jnp.einsum(
        "erh,erd->ehd", up_grad, slot_rows, preferred_element_type=jnp.float32
    ).astype(jnp.bfloat16)
    grad_in = jnp.stack([grad_gate, grad_up], axis=1)
    grad_out = jnp.einsum(
        "erh,erd->ehd", hidden, scaled, preferred_element_type=jnp.float32
    ).astype(jnp.bfloat16)
    return (part_out, input_piece, gate_piece, grad_in, grad_out)


def body(
    first_half,
    second_half,
    first_grad,
    second_grad,
    expert_ids,
    gate_weights,
    expert_in,
    expert_out,
):
    tokens_here = expert_ids.shape[0]
    picks = expert_ids.shape[1]
    groups = lax.axis_size("expert")
    local_count = expert_in.shape[0]
    experts_all = groups * local_count
    capacity = tokens_here * picks * 7 // (6 * experts_all)
    routes = expert_ids.reshape(-1)
    onehot = (routes[:, None] == jnp.arange(experts_all, dtype=jnp.int32)[None, :]).astype(
        jnp.int32
    )
    before = jnp.cumsum(onehot, axis=0) - onehot
    slot_index = jnp.sum(before * onehot, axis=1)
    destination = routes * capacity + slot_index
    route_token = jnp.arange(tokens_here * picks, dtype=jnp.int32) // picks
    slot_token = (
        jnp.full((experts_all * capacity,), tokens_here, jnp.int32).at[destination].set(route_token)
    )
    slot_gate = (
        jnp.zeros((experts_all * capacity,), jnp.bfloat16)
        .at[destination]
        .set(gate_weights.reshape(-1))
    )
    slot_gate = slot_gate.reshape(experts_all, capacity)

    def to_slots(values):
        padded = jnp.concatenate([values, jnp.zeros((1, values.shape[1]), values.dtype)], axis=0)
        return padded[slot_token].reshape(experts_all, capacity, values.shape[1])

    def to_local(values):
        shaped = values.reshape((groups, local_count) + values.shape[1:])
        shaped = jnp.moveaxis(shaped, 1, 0)
        return shaped.reshape((local_count, groups * capacity) + values.shape[2:])

    def to_sources(values):
        shaped = values.reshape((local_count, groups, capacity) + values.shape[2:])
        shaped = jnp.moveaxis(shaped, 0, 1)
        return shaped.reshape((experts_all, capacity) + values.shape[2:])

    whole_first, whole_cots = (
        lax.all_gather(first_half, "tensor", axis=1, tiled=True),
        lax.all_gather(second_grad, "tensor", axis=1, tiled=True),
    )
    recv_rows, recv_cots, recv_gates = (
        lax.all_to_all(to_slots(whole_first), "expert", split_axis=0, concat_axis=0, tiled=True),
        lax.all_to_all(to_slots(whole_cots), "expert", split_axis=0, concat_axis=0, tiled=True),
        lax.all_to_all(slot_gate, "expert", split_axis=0, concat_axis=0, tiled=True),
    )
    results = expert_work(
        to_local(recv_rows), to_local(recv_cots), to_local(recv_gates), expert_in, expert_out
    )
    grad_in = results[3]
    grad_out = results[4]
    gate_all = to_sources(results[2]).astype(jnp.bfloat16)
    weights_f = gate_weights.astype(jnp.float32)
    out_all = to_sources(results[0].astype(jnp.bfloat16))
    input_all = to_sources(results[1].astype(jnp.bfloat16))
    back_out, back_input, back_gate = (
        lax.all_to_all(out_all, "expert", split_axis=0, concat_axis=0, tiled=True),
        lax.all_to_all(input_all, "expert", split_axis=0, concat_axis=0, tiled=True),
        lax.all_to_all(gate_all, "expert", split_axis=0, concat_axis=0, tiled=True),
    )
    width = back_out.shape[2]
    picked_out = back_out.reshape(-1, width)[destination].reshape(tokens_here, picks, width)
    picked_input = back_input.reshape(-1, width)[destination].reshape(tokens_here, picks, width)
    mixed = jnp.sum(weights_f[:, :, None] * picked_out.astype(jnp.float32), axis=1)
    summed_input = jnp.sum(picked_input.astype(jnp.float32), axis=1)
    branch_cols, input_cols = (
        lax.psum_scatter(
            mixed.astype(jnp.bfloat16), "tensor", scatter_dimension=1, tiled=True
        ).astype(jnp.float32),
        lax.psum_scatter(
            summed_input.astype(jnp.bfloat16), "tensor", scatter_dimension=1, tiled=True
        ).astype(jnp.float32),
    )
    gate_back = back_gate.astype(jnp.float32)
    gate_parts = gate_back.reshape(-1)[destination].reshape(tokens_here, picks)
    gate_grad = lax.psum(gate_parts, "tensor")
    restored = (second_half.astype(jnp.float32) - branch_cols).astype(jnp.bfloat16)
    carried_grad = (first_grad.astype(jnp.float32) + input_cols).astype(jnp.bfloat16)
    return (restored, carried_grad, gate_grad, grad_in, grad_out)


def solution(mesh):
    in_specs = (
        P("expert", "tensor"),
        P("expert", "tensor"),
        P("expert", "tensor"),
        P("expert", "tensor"),
        P("expert", None),
        P("expert", None),
        P("expert", None, "tensor", None),
        P("expert", "tensor", None),
    )
    out_specs = (
        P("expert", "tensor"),
        P("expert", "tensor"),
        P("expert", None),
        P("expert", None, "tensor", None),
        P("expert", "tensor", None),
    )
    return jax.shard_map(body, mesh=mesh, in_specs=in_specs, out_specs=out_specs, check_vma=False)
```

profile of v0, /device:TPU:2, one launch (start us, length us, event | category | flops | bytes accessed | tf_op | source)
XLA Modules:
  0.0 958.2 jit_solution(17557005658640460501)
XLA Ops:
  7.2 0.8 broadcast_multiply_fusion
  8.0 0.8 copy.23
  8.7 0.1 eq.29
  8.9 0.1 eq.25
  9.1 0.1 mul.103
  9.3 1.8 reduce-window.6
  11.1 0.3 slice_reduce_fusion
  11.4 0.1 fusion.31
  11.6 3.4 scatter_custom_fusion
  15.0 13.8 %all_gather.6 = bf16[128,2048]{1,0:T(8,128)(2,1)S(1)} all-gather(bf16[128,256]{1,0:T(8,128)(2,1)} %param.8), channel_id=1, replica_groups=mesh['expert'=64,'tensor'=8] {'tensor'}, dimensions={1}, use_global_device_ids=true | all-gather | bytes 589824 | tf_op jit(solution)/shard_map/all_gather | solution.py:91
  28.9 5.0 gather_fusion
  33.9 6.0 reshape.268
  39.9 19.0 %all-to-all-start = ((bf16[64,14,2048]{2,1,0:T(8,128)(2,1)}), bf16[64,14,2048]{2,1,0:T(8,128)(2,1)}, u32[]{:S(2)}, u32[]{:S(2)}) async-start(bf16[64,14,2048]{2,1,0:T(8,128)(2,1)} %reshape.268), calls=%async_computation | async-start | bytes 8388608 | tf_op jit(solution)/shard_map/all_to_all | solution.py:95
  58.9 13.1 %all_gather.7 = bf16[128,2048]{1,0:T(8,128)(2,1)S(1)} all-gather(bf16[128,256]{1,0:T(8,128)(2,1)S(1)} %copy-done.4), channel_id=1, replica_groups=mesh['expert'=64,'tensor'=8] {'tensor'}, dimensions={1}, use_global_device_ids=true | all-gather | bytes 589824 | tf_op jit(solution)/shard_map/all_gather | solution.py:92
  72.0 5.1 gather_fusion.2
  77.1 6.0 reshape.274
  83.1 162.1 %all-to-all-done = bf16[64,14,2048]{2,1,0:T(8,128)(2,1)} async-done(((bf16[64,14,2048]{2,1,0:T(8,128)(2,1)}), bf16[64,14,2048]{2,1,0:T(8,128)(2,1)}, u32[]{:S(2)}, u32[]{:S(2)}) %all-to-all-start) | async-done | bytes 3670048 | tf_op jit(solution)/shard_map/all_to_all | solution.py:95
  245.2 10.5 %all-to-all-start.3 = ((bf16[64,14,2048]{2,1,0:T(8,128)(2,1)}), bf16[64,14,2048]{2,1,0:T(8,128)(2,1)}, u32[]{:S(2)}, u32[]{:S(2)}) async-start(bf16[64,14,2048]{2,1,0:T(8,128)(2,1)} %reshape.274), calls=%async_computation.4 | async-start | bytes 8388608 | tf_op jit(solution)/shard_map/all_to_all | solution.py:96
  255.7 0.1 copy.26
  255.8 0.2 reshape.337
  256.0 8.6 scatter_custom_fusion.1
  264.6 0.8 all_to_all.29
  265.4 6.1 reshape.343
  271.5 3.7 fusion.6
  275.2 1.0 copy-done.3
  276.2 0.2 multiply_convert_fusion.1
  276.4 164.4 %all-to-all-done.3 = bf16[64,14,2048]{2,1,0:T(8,128)(2,1)} async-done(((bf16[64,14,2048]{2,1,0:T(8,128)(2,1)}), bf16[64,14,2048]{2,1,0:T(8,128)(2,1)}, u32[]{:S(2)}, u32[]{:S(2)}) %all-to-all-start.3) | async-done | bytes 3670048 | tf_op jit(solution)/shard_map/all_to_all | solution.py:96
  440.8 9.9 %all-to-all-start.2 = ((bf16[64,1,14]{2,1,0:T(2,128)(2,1)}), bf16[64,1,14]{2,1,0:T(2,128)(2,1)S(1)}, u32[]{:S(2)}, u32[]{:S(2)}) async-start(bf16[64,1,14]{2,1,0:T(2,128)(2,1)} %all_to_all.29), calls=%async_computation.3 | async-start | bytes 65536 | tf_op jit(solution)/shard_map/all_to_all | solution.py:97
  450.7 6.5 reshape.283
  457.1 6.1 multiply_reduce_fusion.1
  463.3 6.0 reshape_transpose_reshape.4
  469.3 15.7 %all-to-all-start.1 = ((bf16[64,14,2048]{2,1,0:T(8,128)(2,1)}), bf16[64,14,2048]{2,1,0:T(8,128)(2,1)}, u32[]{:S(2)}, u32[]{:S(2)}) async-start(bf16[64,14,2048]{2,1,0:T(8,128)(2,1)} %reshape_transpose_reshape.4), calls=%async_computation.1 | async-start | bytes 8388608 | tf_op jit(solution)/shard_map/all_to_all | solution.py:109
  485.1 0.1 reshape.281
  485.2 6.4 reshape.282
  491.6 4.9 fusion.25
  496.5 1.2 fusion.10
  497.6 3.1 add_convert_fusion
  500.7 6.0 reshape_transpose_reshape.10
  506.8 162.8 %all-to-all-done.1 = bf16[64,14,2048]{2,1,0:T(8,128)(2,1)} async-done(((bf16[64,14,2048]{2,1,0:T(8,128)(2,1)}), bf16[64,14,2048]{2,1,0:T(8,128)(2,1)}, u32[]{:S(2)}, u32[]{:S(2)}) %all-to-all-start.1) | async-done | bytes 3670048 | tf_op jit(solution)/shard_map/all_to_all | solution.py:109
  669.5 10.1 %all-to-all-start.4 = ((bf16[64,14,2048]{2,1,0:T(8,128)(2,1)}), bf16[64,14,2048]{2,1,0:T(8,128)(2,1)}, u32[]{:S(2)}, u32[]{:S(2)}) async-start(bf16[64,14,2048]{2,1,0:T(8,128)(2,1)} %reshape_transpose_reshape.10), calls=%async_computation.5 | async-start | bytes 8388608 | tf_op jit(solution)/shard_map/all_to_all | solution.py:110
  679.8 6.0 reshape.272
  685.8 9.6 %gather_fusion.1 = bf16[768,2048]{1,0:T(8,128)(2,1)} fusion(bf16[896,2048]{1,0:T(8,128)(2,1)} %reshape.272, s32[1024]{0:T(1024)S(1)} %pad_clamp_fusion), kind=kCustom, calls=%fused_computation.1 | custom fusion | bytes 6294528 | tf_op jit(solution)/shard_map/gather | solution.py:114
  695.4 6.6 reshape.280
  702.0 7.4 multiply_reduce_fusion
  709.4 0.3 reduce-scatter.5.cloned.1.call-start
  709.6 6.0 reshape.269
  715.6 3.0 fusion.2
  718.6 146.4 %all-to-all-done.4 = bf16[64,14,2048]{2,1,0:T(8,128)(2,1)} async-done(((bf16[64,14,2048]{2,1,0:T(8,128)(2,1)}), bf16[64,14,2048]{2,1,0:T(8,128)(2,1)}, u32[]{:S(2)}, u32[]{:S(2)}) %all-to-all-start.4) | async-done | bytes 3670048 | tf_op jit(solution)/shard_map/all_to_all | solution.py:110
  865.1 6.0 reshape.277
  871.1 9.7 %gather_fusion.3 = bf16[768,2048]{1,0:T(8,128)(2,1)} fusion(bf16[896,2048]{1,0:T(8,128)(2,1)} %reshape.277, s32[1024]{0:T(1024)S(1)} %pad_clamp_fusion), kind=kCustom, calls=%fused_computation.3 | custom fusion | bytes 6294528 | tf_op jit(solution)/shard_map/gather | solution.py:115
  880.7 6.3 reshape.278
  887.0 5.7 reduce_sum.44
  892.7 3.0 fusion.1
  895.7 0.8 convert_element_type.209
  896.5 10.0 %all-to-all-start.5 = ((bf16[64,1,14]{2,1,0:T(2,128)(2,1)}), bf16[64,1,14]{2,1,0:T(2,128)(2,1)S(1)}, u32[]{:S(2)}, u32[]{:S(2)}) async-start(bf16[64,1,14]{2,1,0:T(2,128)(2,1)} %convert_element_type.209), calls=%async_computation.7 | async-start | bytes 65536 | tf_op jit(solution)/shard_map/all_to_all | solution.py:111
  906.5 5.0 fusion.3
  911.5 1.2 pad_maximum_fusion
  912.7 7.2 all-to-all-done.5
  920.0 0.1 reshape.284
  920.1 3.2 gather_fusion.4
  923.5 24.0 %psum.7 = f32[128,6]{1,0:T(8,128)S(1)} all-reduce(f32[128,6]{1,0:T(8,128)S(1)} %reshape.279), channel_id=1, replica_groups=mesh['expert'=64,'tensor'=8] {'tensor'}, use_global_device_ids=true, to_apply=%region_10.11 | all-reduce | flops 768 | bytes 6144 | tf_op jit(solution)/shard_map/psum | solution.py:128
  947.5 0.7 copy.29
  948.1 1.5 subtract_convert_fusion
  949.6 1.5 add_convert_fusion.1
  (35 shorter events, 0.8 us)
Async XLA Ops:
  7.2 450.0 %copy-start = (bf16[1,176,2048]{2,1,0:T(8,128)(2,1)S(1)}, bf16[1,176,2048]{2,1,0:T(8,128)(2,1)}, u32[]{:S(2)}) copy-start(bf16[1,176,2048]{2,1,0:T(8,128)(2,1)} %param.15) | copy-start | bytes 2162692
  39.9 19.0 %copy-start.4 = (bf16[128,256]{1,0:T(8,128)(2,1)S(1)}, bf16[128,256]{1,0:T(8,128)(2,1)}, u32[]{:S(2)}) copy-start(bf16[128,256]{1,0:T(8,128)(2,1)} %param.11) | copy-start | bytes 196612
  39.9 205.3 %all-to-all-start = ((bf16[64,14,2048]{2,1,0:T(8,128)(2,1)}), bf16[64,14,2048]{2,1,0:T(8,128)(2,1)}, u32[]{:S(2)}, u32[]{:S(2)}) async-start(bf16[64,14,2048]{2,1,0:T(8,128)(2,1)} %reshape.268), calls=%async_computation | async-start | bytes 8388608 | tf_op jit(solution)/shard_map/all_to_all | solution.py:95
  83.1 172.6 %copy-start.7 = (bf16[128,6]{0,1:T(8,128)(2,1)S(1)}, bf16[128,6]{0,1:T(8,128)(2,1)}, u32[]{:S(2)}) copy-start(bf16[128,6]{0,1:T(8,128)(2,1)} %param.13) | copy-start | bytes 4612
  245.2 195.6 %all-to-all-start.3 = ((bf16[64,14,2048]{2,1,0:T(8,128)(2,1)}), bf16[64,14,2048]{2,1,0:T(8,128)(2,1)}, u32[]{:S(2)}, u32[]{:S(2)}) async-start(bf16[64,14,2048]{2,1,0:T(8,128)(2,1)} %reshape.274), calls=%async_computation.4 | async-start | bytes 8388608 | tf_op jit(solution)/shard_map/all_to_all | solution.py:96
  265.4 6.1 copy-start.2
  275.2 1.0 copy-start.3
  440.8 28.5 %all-to-all-start.2 = ((bf16[64,1,14]{2,1,0:T(2,128)(2,1)}), bf16[64,1,14]{2,1,0:T(2,128)(2,1)S(1)}, u32[]{:S(2)}, u32[]{:S(2)}) async-start(bf16[64,1,14]{2,1,0:T(2,128)(2,1)} %all_to_all.29), calls=%async_computation.3 | async-start | bytes 65536 | tf_op jit(solution)/shard_map/all_to_all | solution.py:97
  469.3 200.3 %all-to-all-start.1 = ((bf16[64,14,2048]{2,1,0:T(8,128)(2,1)}), bf16[64,14,2048]{2,1,0:T(8,128)(2,1)}, u32[]{:S(2)}, u32[]{:S(2)}) async-start(bf16[64,14,2048]{2,1,0:T(8,128)(2,1)} %reshape_transpose_reshape.4), calls=%async_computation.1 | async-start | bytes 8388608 | tf_op jit(solution)/shard_map/all_to_all | solution.py:109
  669.5 195.5 %all-to-all-start.4 = ((bf16[64,14,2048]{2,1,0:T(8,128)(2,1)}), bf16[64,14,2048]{2,1,0:T(8,128)(2,1)}, u32[]{:S(2)}, u32[]{:S(2)}) async-start(bf16[64,14,2048]{2,1,0:T(8,128)(2,1)} %reshape_transpose_reshape.10), calls=%async_computation.5 | async-start | bytes 8388608 | tf_op jit(solution)/shard_map/all_to_all | solution.py:110
  679.6 268.5 %reduce-scatter.3.cloned.1.call-start = ((), (), s32[]{:S(2)}) async-start(), calls=%async_computation.8 | async-start | bytes 589824 | tf_op jit(solution)/shard_map/reduce_scatter | solution.py:119
  709.4 240.3 %reduce-scatter.5.cloned.1.call-start = ((), (), s32[]{:S(2)}) async-start(), calls=%async_computation.9 | async-start | bytes 589824 | tf_op jit(solution)/shard_map/reduce_scatter | solution.py:122
  896.5 23.4 %all-to-all-start.5 = ((bf16[64,1,14]{2,1,0:T(2,128)(2,1)}), bf16[64,1,14]{2,1,0:T(2,128)(2,1)S(1)}, u32[]{:S(2)}, u32[]{:S(2)}) async-start(bf16[64,1,14]{2,1,0:T(2,128)(2,1)} %convert_element_type.209), calls=%async_computation.7 | async-start | bytes 65536 | tf_op jit(solution)/shard_map/all_to_all | solution.py:111
  906.4 44.7 %copy-start.1 = (bf16[1,176,2048]{2,1,0:T(8,128)(2,1)S(1)}, bf16[1,176,2048]{2,1,0:T(8,128)(2,1)}, u32[]{:S(2)}) copy-start(bf16[1,176,2048]{2,1,0:T(8,128)(2,1)} %param.15) | copy-start | bytes 2162692
  911.5 36.7 %copy-start.5 = (bf16[128,256]{1,0:T(8,128)(2,1)S(1)}, bf16[128,256]{1,0:T(8,128)(2,1)}, u32[]{:S(2)}) copy-start(bf16[128,256]{1,0:T(8,128)(2,1)} %param.9) | copy-start | bytes 196612
  911.5 38.1 %copy-start.6 = (bf16[128,256]{1,0:T(8,128)(2,1)S(1)}, bf16[128,256]{1,0:T(8,128)(2,1)}, u32[]{:S(2)}) copy-start(bf16[128,256]{1,0:T(8,128)(2,1)} %param.10) | copy-start | bytes 196612
Sparse Core Ops, SparseCore 0:
  709.5 39.6 reduce-scatter.2
  892.8 34.0 reduce-scatter.4
where the time goes:
time: 967 us; the launch traced here: 958 us
  waiting for transfers between devices  643 us (66%)
  local copies, waits for them, and re-layouts  124 us (13%)
  starting transfers between devices  75.4 us (8%)
  blocking collectives  50.9 us (5%)
  matrix products  30 us (3%)
  other arithmetic  20.4 us (2%)
  between operations  14.6 us (2%)
    all_to_all x1, waiting for transfers between devices, body(): lax.all_to_all(to_slots(whole_cots), 'expert', split_axis=0, concat_axis=...  164 us
    all_to_all x1, waiting for transfers between devices, body(): lax.all_to_all(out_all, 'expert', split_axis=0, concat_axis=0, tiled=True)  163 us
    all_to_all x1, waiting for transfers between devices, body(): lax.all_to_all(to_slots(whole_first), 'expert', split_axis=0, concat_axis...  162 us
    all_to_all x1, waiting for transfers between devices, body(): lax.all_to_all(input_all, 'expert', split_axis=0, concat_axis=0, tiled=True)  146 us
    psum x1, blocking collectives, body(): gate_grad = lax.psum(gate_parts, 'tensor')  24 us
  transfers between devices with their start and end apart: 8, of which 5 were waited for; matrix products, arithmetic and copies ran while one was open for 16% of the time, Pallas kernels for 0%

commit v1 on v0

--- a/solution.py
+++ b/solution.py
@@ -125,7 +125,11 @@
     )
     gate_back = back_gate.astype(jnp.float32)
     gate_parts = gate_back.reshape(-1)[destination].reshape(tokens_here, picks)
-    gate_grad = lax.psum(gate_parts, "tensor")
+    gate_grad = gate_parts
+    for hop in (1, 2, 4):
+        gate_grad = gate_grad + lax.ppermute(
+            gate_grad, "tensor", [(dev, dev ^ hop) for dev in range(8)]
+        )
     restored = (second_half.astype(jnp.float32) - branch_cols).astype(jnp.bfloat16)
     carried_grad = (first_grad.astype(jnp.float32) + input_cols).astype(jnp.bfloat16)
     return (restored, carried_grad, gate_grad, grad_in, grad_out)

time: 967 us -> 959 us (level)
  the two profiles are of different devices: /device:TPU:2 before, /device:TPU:6 now
where the time goes in v1:
time: 959 us; the launch traced here: 951 us
  waiting for transfers between devices  654 us (68%)
  local copies, waits for them, and re-layouts  124 us (13%)
  starting transfers between devices  83.1 us (9%)
  matrix products  28 us (3%)
  blocking collectives  27 us (3%)
  other arithmetic  20.5 us (2%)
  between operations  14.6 us (2%)
    all_to_all x1, waiting for transfers between devices, body(): lax.all_to_all(to_slots(whole_cots), 'expert', split_axis=0, concat_axis=...  165 us
    all_to_all x1, waiting for transfers between devices, body(): lax.all_to_all(out_all, 'expert', split_axis=0, concat_axis=0, tiled=True)  162 us
    all_to_all x1, waiting for transfers between devices, body(): lax.all_to_all(to_slots(whole_first), 'expert', split_axis=0, concat_axis...  162 us
    all_to_all x1, waiting for transfers between devices, body(): lax.all_to_all(input_all, 'expert', split_axis=0, concat_axis=0, tiled=True)  139 us
  transfers between devices with their start and end apart: 11, of which 8 were waited for; matrix products, arithmetic and copies ran while one was open for 16% of the time, Pallas kernels for 0%

profile of v1, /device:TPU:6, one launch (start us, length us, event | category | flops | bytes accessed | tf_op | source)
XLA Modules:
  0.0 951.1 jit_solution(7592759160706919970)
XLA Ops:
  7.2 0.8 broadcast_multiply_fusion
  8.0 0.8 copy.23
  9.1 0.1 mul.103
  9.3 1.8 reduce-window.6
  11.1 0.3 slice_reduce_fusion
  11.6 3.4 scatter_custom_fusion
  15.0 13.8 %all_gather.6 = bf16[128,2048]{1,0:T(8,128)(2,1)S(1)} all-gather(bf16[128,256]{1,0:T(8,128)(2,1)} %param.8), channel_id=1, replica_groups=mesh['expert'=64,'tensor'=8] {'tensor'}, dimensions={1}, use_global_device_ids=true | all-gather | bytes 589824 | tf_op jit(solution)/shard_map/all_gather | solution.py:91
  28.9 5.0 gather_fusion
  33.9 6.0 reshape.268
  39.9 19.1 %all-to-all-start = ((bf16[64,14,2048]{2,1,0:T(8,128)(2,1)}), bf16[64,14,2048]{2,1,0:T(8,128)(2,1)}, u32[]{:S(2)}, u32[]{:S(2)}) async-start(bf16[64,14,2048]{2,1,0:T(8,128)(2,1)} %reshape.268), calls=%async_computation | async-start | bytes 8388608 | tf_op jit(solution)/shard_map/all_to_all | solution.py:95
  59.0 13.1 %all_gather.7 = bf16[128,2048]{1,0:T(8,128)(2,1)S(1)} all-gather(bf16[128,256]{1,0:T(8,128)(2,1)S(1)} %copy-done.5), channel_id=1, replica_groups=mesh['expert'=64,'tensor'=8] {'tensor'}, dimensions={1}, use_global_device_ids=true | all-gather | bytes 589824 | tf_op jit(solution)/shard_map/all_gather | solution.py:92
  72.2 5.1 gather_fusion.2
  77.2 6.0 reshape.274
  83.3 162.1 %all-to-all-done = bf16[64,14,2048]{2,1,0:T(8,128)(2,1)} async-done(((bf16[64,14,2048]{2,1,0:T(8,128)(2,1)}), bf16[64,14,2048]{2,1,0:T(8,128)(2,1)}, u32[]{:S(2)}, u32[]{:S(2)}) %all-to-all-start) | async-done | bytes 3670048 | tf_op jit(solution)/shard_map/all_to_all | solution.py:95
  245.4 10.5 %all-to-all-start.3 = ((bf16[64,14,2048]{2,1,0:T(8,128)(2,1)}), bf16[64,14,2048]{2,1,0:T(8,128)(2,1)}, u32[]{:S(2)}, u32[]{:S(2)}) async-start(bf16[64,14,2048]{2,1,0:T(8,128)(2,1)} %reshape.274), calls=%async_computation.4 | async-start | bytes 8388608 | tf_op jit(solution)/shard_map/all_to_all | solution.py:96
  255.9 0.1 copy.26
  256.0 0.2 reshape.337
  256.1 8.6 scatter_custom_fusion.1
  264.8 0.8 all_to_all.29
  265.5 6.1 reshape.343
  271.6 3.7 fusion.6
  275.4 1.0 copy-done.4
  276.4 0.2 multiply_convert_fusion.1
  276.6 164.6 %all-to-all-done.3 = bf16[64,14,2048]{2,1,0:T(8,128)(2,1)} async-done(((bf16[64,14,2048]{2,1,0:T(8,128)(2,1)}), bf16[64,14,2048]{2,1,0:T(8,128)(2,1)}, u32[]{:S(2)}, u32[]{:S(2)}) %all-to-all-start.3) | async-done | bytes 3670048 | tf_op jit(solution)/shard_map/all_to_all | solution.py:96
  441.1 9.6 %all-to-all-start.2 = ((bf16[64,1,14]{2,1,0:T(2,128)(2,1)}), bf16[64,1,14]{2,1,0:T(2,128)(2,1)S(1)}, u32[]{:S(2)}, u32[]{:S(2)}) async-start(bf16[64,1,14]{2,1,0:T(2,128)(2,1)} %all_to_all.29), calls=%async_computation.3 | async-start | bytes 65536 | tf_op jit(solution)/shard_map/all_to_all | solution.py:97
  450.8 6.5 reshape.283
  457.3 6.1 multiply_reduce_fusion.1
  463.4 0.8 convert_element_type.209
  464.2 15.1 %all-to-all-start.5 = ((bf16[64,1,14]{2,1,0:T(2,128)(2,1)}), bf16[64,1,14]{2,1,0:T(2,128)(2,1)S(1)}, u32[]{:S(2)}, u32[]{:S(2)}) async-start(bf16[64,1,14]{2,1,0:T(2,128)(2,1)} %convert_element_type.209), calls=%async_computation.7 | async-start | bytes 65536 | tf_op jit(solution)/shard_map/all_to_all | solution.py:111
  479.3 6.0 reshape_transpose_reshape.4
  485.3 6.5 all-to-all-done.5
  491.8 9.2 all-to-all-start.1
  501.3 6.4 reshape.282
  507.7 4.8 fusion.25
  512.5 1.2 fusion.10
  513.7 3.1 add_convert_fusion
  516.8 6.0 reshape_transpose_reshape.10
  522.8 162.3 %all-to-all-done.1 = bf16[64,14,2048]{2,1,0:T(8,128)(2,1)} async-done(((bf16[64,14,2048]{2,1,0:T(8,128)(2,1)}), bf16[64,14,2048]{2,1,0:T(8,128)(2,1)}, u32[]{:S(2)}, u32[]{:S(2)}) %all-to-all-start.1) | async-done | bytes 3670048 | tf_op jit(solution)/shard_map/all_to_all | solution.py:109
  685.1 10.0 %all-to-all-start.4 = ((bf16[64,14,2048]{2,1,0:T(8,128)(2,1)}), bf16[64,14,2048]{2,1,0:T(8,128)(2,1)}, u32[]{:S(2)}, u32[]{:S(2)}) async-start(bf16[64,14,2048]{2,1,0:T(8,128)(2,1)} %reshape_transpose_reshape.10), calls=%async_computation.5 | async-start | bytes 8388608 | tf_op jit(solution)/shard_map/all_to_all | solution.py:110
  695.3 6.0 reshape.272
  701.3 9.6 %gather_fusion.1 = bf16[768,2048]{1,0:T(8,128)(2,1)} fusion(bf16[896,2048]{1,0:T(8,128)(2,1)} %reshape.272, s32[1024]{0:T(1024)S(1)} %pad_clamp_fusion), kind=kCustom, calls=%fused_computation.1 | custom fusion | bytes 6294528 | tf_op jit(solution)/shard_map/gather | solution.py:114
  710.9 6.6 reshape.280
  717.5 7.4 multiply_reduce_fusion
  724.9 0.3 reduce-scatter.5.cloned.1.call-start
  725.1 6.0 reshape.269
  731.1 4.9 fusion.3
  736.3 3.2 gather_fusion.4
  739.6 1.9 collective-permute-start
  741.6 139.3 %all-to-all-done.4 = bf16[64,14,2048]{2,1,0:T(8,128)(2,1)} async-done(((bf16[64,14,2048]{2,1,0:T(8,128)(2,1)}), bf16[64,14,2048]{2,1,0:T(8,128)(2,1)}, u32[]{:S(2)}, u32[]{:S(2)}) %all-to-all-start.4) | async-done | bytes 3670048 | tf_op jit(solution)/shard_map/all_to_all | solution.py:110
  880.8 6.0 reshape.277
  886.8 9.6 %gather_fusion.3 = bf16[768,2048]{1,0:T(8,128)(2,1)} fusion(bf16[896,2048]{1,0:T(8,128)(2,1)} %reshape.277, s32[1024]{0:T(1024)S(1)} %pad_clamp_fusion), kind=kCustom, calls=%fused_computation.3 | custom fusion | bytes 6294528 | tf_op jit(solution)/shard_map/gather | solution.py:115
  896.5 6.3 reshape.278
  902.7 5.7 reduce_sum.44
  908.4 3.1 fusion.2
  911.7 3.3 collective-permute-start.1
  915.0 1.0 fusion.1
  916.0 2.5 collective-permute-done.1
  918.4 4.0 collective-permute-start.2
  922.4 1.2 pad_maximum_fusion
  923.7 2.8 collective-permute-done.2
  926.5 0.7 copy.29
  927.1 1.5 subtract_convert_fusion
  928.6 13.9 %reduce-scatter.5.cloned.1.call-done = bf16[128,256]{1,0:T(8,128)(2,1)} async-done(((bf16[128,2048]{1,0:T(8,128)(2,1)}), bf16[128,256]{1,0:T(8,128)(2,1)}) %reduce-scatter.5.cloned.1.call-update) | async-done | bytes 65552 | tf_op jit(solution)/shard_map/reduce_scatter | solution.py:122
  942.5 1.5 add_convert_fusion.1
  (45 shorter events, 1.5 us)
Async XLA Ops:
  7.2 450.1 %copy-start = (bf16[1,176,2048]{2,1,0:T(8,128)(2,1)S(1)}, bf16[1,176,2048]{2,1,0:T(8,128)(2,1)}, u32[]{:S(2)}) copy-start(bf16[1,176,2048]{2,1,0:T(8,128)(2,1)} %param.15) | copy-start | bytes 2162692
  39.9 19.1 %copy-start.5 = (bf16[128,256]{1,0:T(8,128)(2,1)S(1)}, bf16[128,256]{1,0:T(8,128)(2,1)}, u32[]{:S(2)}) copy-start(bf16[128,256]{1,0:T(8,128)(2,1)} %param.11) | copy-start | bytes 196612
  39.9 205.5 %all-to-all-start = ((bf16[64,14,2048]{2,1,0:T(8,128)(2,1)}), bf16[64,14,2048]{2,1,0:T(8,128)(2,1)}, u32[]{:S(2)}, u32[]{:S(2)}) async-start(bf16[64,14,2048]{2,1,0:T(8,128)(2,1)} %reshape.268), calls=%async_computation | async-start | bytes 8388608 | tf_op jit(solution)/shard_map/all_to_all | solution.py:95
  83.2 172.6 %copy-start.8 = (bf16[128,6]{0,1:T(8,128)(2,1)S(1)}, bf16[128,6]{0,1:T(8,128)(2,1)}, u32[]{:S(2)}) copy-start(bf16[128,6]{0,1:T(8,128)(2,1)} %param.13) | copy-start | bytes 4612
  245.4 195.8 %all-to-all-start.3 = ((bf16[64,14,2048]{2,1,0:T(8,128)(2,1)}), bf16[64,14,2048]{2,1,0:T(8,128)(2,1)}, u32[]{:S(2)}, u32[]{:S(2)}) async-start(bf16[64,14,2048]{2,1,0:T(8,128)(2,1)} %reshape.274), calls=%async_computation.4 | async-start | bytes 8388608 | tf_op jit(solution)/shard_map/all_to_all | solution.py:96
  265.5 6.1 copy-start.3
  275.3 1.0 copy-start.4
  441.1 23.0 %all-to-all-start.2 = ((bf16[64,1,14]{2,1,0:T(2,128)(2,1)}), bf16[64,1,14]{2,1,0:T(2,128)(2,1)S(1)}, u32[]{:S(2)}, u32[]{:S(2)}) async-start(bf16[64,1,14]{2,1,0:T(2,128)(2,1)} %all_to_all.29), calls=%async_computation.3 | async-start | bytes 65536 | tf_op jit(solution)/shard_map/all_to_all | solution.py:97
  464.2 27.6 %all-to-all-start.5 = ((bf16[64,1,14]{2,1,0:T(2,128)(2,1)}), bf16[64,1,14]{2,1,0:T(2,128)(2,1)S(1)}, u32[]{:S(2)}, u32[]{:S(2)}) async-start(bf16[64,1,14]{2,1,0:T(2,128)(2,1)} %convert_element_type.209), calls=%async_computation.7 | async-start | bytes 65536 | tf_op jit(solution)/shard_map/all_to_all | solution.py:111
  491.8 193.3 %all-to-all-start.1 = ((bf16[64,14,2048]{2,1,0:T(8,128)(2,1)}), bf16[64,14,2048]{2,1,0:T(8,128)(2,1)}, u32[]{:S(2)}, u32[]{:S(2)}) async-start(bf16[64,14,2048]{2,1,0:T(8,128)(2,1)} %reshape_transpose_reshape.4), calls=%async_computation.1 | async-start | bytes 8388608 | tf_op jit(solution)/shard_map/all_to_all | solution.py:109
  685.1 195.7 %all-to-all-start.4 = ((bf16[64,14,2048]{2,1,0:T(8,128)(2,1)}), bf16[64,14,2048]{2,1,0:T(8,128)(2,1)}, u32[]{:S(2)}, u32[]{:S(2)}) async-start(bf16[64,14,2048]{2,1,0:T(8,128)(2,1)} %reshape_transpose_reshape.10), calls=%async_computation.5 | async-start | bytes 8388608 | tf_op jit(solution)/shard_map/all_to_all | solution.py:110
  695.1 232.0 %reduce-scatter.3.cloned.1.call-start = ((), (), s32[]{:S(2)}) async-start(), calls=%async_computation.8 | async-start | bytes 589824 | tf_op jit(solution)/shard_map/reduce_scatter | solution.py:119
  724.9 217.6 %reduce-scatter.5.cloned.1.call-start = ((), (), s32[]{:S(2)}) async-start(), calls=%async_computation.9 | async-start | bytes 589824 | tf_op jit(solution)/shard_map/reduce_scatter | solution.py:122
  739.6 172.0 %collective-permute-start = (f32[128,6]{1,0:T(8,128)S(1)}, f32[128,6]{1,0:T(8,128)S(1)}, u32[]{:S(2)}, u32[]{:S(2)}) collective-permute-start(f32[128,6]{1,0:T(8,128)S(1)} %reshape.279), channel_id=1, source_target_pairs={{0,1},{1,0},{2,3},{3,2},{4,5},{5,4},{6,7},{7,6},{8,9},{9,8},{10,11... | collective-permute-start | bytes 9224 | tf_op jit(solution)/shard_map/ppermute | solution.py:130
  908.4 6.6 copy-start.2
  911.6 32.4 %copy-start.1 = (bf16[1,176,2048]{2,1,0:T(8,128)(2,1)S(1)}, bf16[1,176,2048]{2,1,0:T(8,128)(2,1)}, u32[]{:S(2)}) copy-start(bf16[1,176,2048]{2,1,0:T(8,128)(2,1)} %param.15) | copy-start | bytes 2162692
  911.6 15.5 %copy-start.6 = (bf16[128,256]{1,0:T(8,128)(2,1)S(1)}, bf16[128,256]{1,0:T(8,128)(2,1)}, u32[]{:S(2)}) copy-start(bf16[128,256]{1,0:T(8,128)(2,1)} %param.9) | copy-start | bytes 196612
  911.6 30.9 %copy-start.7 = (bf16[128,256]{1,0:T(8,128)(2,1)S(1)}, bf16[128,256]{1,0:T(8,128)(2,1)}, u32[]{:S(2)}) copy-start(bf16[128,256]{1,0:T(8,128)(2,1)} %param.10) | copy-start | bytes 196612
  911.7 6.8 collective-permute-start.1
  918.4 8.0 collective-permute-start.2
Sparse Core Ops, SparseCore 0:
  725.0 39.5 reduce-scatter.2
  908.6 33.9 reduce-scatter.4
